TPU v7x, 32 devices: a whole 2x2x4 slice. The times are simulated.
32 devices in a mesh: grp: 2 (over y), seq: 4 (over z), blk: 2 (over x), rep: 2 (over core).
Axes of the slice: x: 2, y: 2, z: 4, core: 2. Of those that a mesh axis runs over, the one named last changes fastest.
Arguments:
- q_proj: bfloat16 [8, 2048, 512], P(('grp', 'blk', 'rep'), 'seq'), parts along dimension 0, may hold values from -6 to 6
- k_proj: bfloat16 [8, 2048, 128], P(('grp', 'blk', 'rep'), 'seq'), parts along dimension 0, may hold values from -6 to 6
- v_proj: bfloat16 [8, 2048, 128], P(('grp', 'blk', 'rep'), 'seq'), parts along dimension 0, may hold values from -6 to 6
- q_gain: float32 [128], replicated, may hold values from 0.5 to 1.5
- k_gain: float32 [128], replicated, may hold values from 0.5 to 1.5
- out_weight: bfloat16 [512, 2560], P('seq'), may hold values from -0.25 to 0.25
- lengths: int32 [8, 1], P(('grp', 'blk', 'rep')), parts along dimension 0, may hold values from 512 to 2048, as said below
- query_emb: bfloat16 [512, 2560], P(('grp', 'blk')), parts along dimension 0, may hold values from -6 to 6
- teacher: float32 [512, 4], P(('grp', 'blk')), parts along dimension 0, may hold values from -16 to 16
Outputs:
- q_grad: bfloat16 [8, 2048, 512], P(('grp', 'blk', 'rep'), 'seq'), parts along dimension 0
- k_grad: bfloat16 [8, 2048, 128], P(('grp', 'blk', 'rep'), 'seq'), parts along dimension 0
- v_grad: bfloat16 [8, 2048, 128], P(('grp', 'blk', 'rep'), 'seq'), parts along dimension 0
- weight_grad: bfloat16 [1024, 2560], P(('grp', 'seq')), parts along dimension 0
- row_loss: float32 [512], P(('grp', 'blk')), parts along dimension 0
- col_loss: float32 [8], P('grp'), parts along dimension 0
There are 2 independent parts, one for each index of `grp`. A program takes and returns all parts, laid end to end along the dimension named above; an argument that names none is the same for every part. Nothing has to cross between parts.
Inputs may be any that keep to these rules, and one draw needn't show every extreme that they name: `lengths`: live tokens of each passage, counted from its first position; the rest is padding.
All inputs are finite; a program needn't handle non-finite values.
Results may differ from a plain program's by a relative error of at most 0.017.
Values may be sent and summed in bfloat16 or wider, within the bound.
A program may use at most 64 MiB of HBM per device.

v0:
```python
import math
import jax
import jax.numpy as jnp
from jax import lax
from jax.sharding import PartitionSpec as P

HD = 128
PASS_LEN = 2048
logit_divisor = 0.05


def rms_scale(wide):
    return lax.rsqrt(jnp.mean(wide * wide, axis=-1, keepdims=True) + 1e-06)


def normed(source, gain_weights):
    wide = source.astype(jnp.float32)
    return (wide * rms_scale(wide) * gain_weights).astype(jnp.bfloat16)


def norm_back(source, gain_weights, grad_out):
    wide = source.astype(jnp.float32)
    inv_rms = rms_scale(wide)
    scaled_grad = gain_weights * grad_out
    return (
        inv_rms * scaled_grad
        - wide * inv_rms**3 * jnp.mean(scaled_grad * wide, axis=-1, keepdims=True)
    ).astype(jnp.bfloat16)


def shards(q_proj, k_proj, v_proj, q_gain, k_gain, out_weight, lengths, query_emb, teacher):
    number_of_sequences = lax.axis_size("seq")
    blk_count = lax.axis_size("blk")
    tok_dev = q_proj.shape[1]
    heads_all = q_proj.shape[2] // HD
    kv_heads = k_proj.shape[2] // HD
    group_size = heads_all // kv_heads
    local_heads = out_weight.shape[0] // HD
    group_tok = tok_dev * number_of_sequences
    passes = group_tok // PASS_LEN
    pass_lens = lengths[0]
    inv_root = 1.0 / math.sqrt(HD)
    block_rows = min(512, PASS_LEN)
    block_count = PASS_LEN // block_rows

    def widen(rows):
        spread = jnp.broadcast_to(
            rows.reshape(tok_dev, kv_heads, 1, HD), (tok_dev, kv_heads, group_size, HD)
        )
        return spread.reshape(tok_dev, heads_all * HD)

    q_heads, k_heads, v_heads = (
        lax.all_to_all(q_proj[0], "seq", split_axis=1, concat_axis=0, tiled=True),
        lax.all_to_all(widen(k_proj[0]), "seq", split_axis=1, concat_axis=0, tiled=True),
        lax.all_to_all(widen(v_proj[0]), "seq", split_axis=1, concat_axis=0, tiled=True),
    )
    head_shape = (passes, PASS_LEN, local_heads, HD)
    q_raw = q_heads.reshape(head_shape)
    k_raw = k_heads.reshape(head_shape)
    v_all = v_heads.reshape(head_shape)
    q_unit = normed(q_raw, q_gain)
    k_unit = normed(k_raw, k_gain)
    positions = lax.iota(jnp.int32, PASS_LEN)
    passage = 0
    q_block = q_unit[passage]
    k_block = k_unit[passage]
    stored = []
    for attend_index in range(block_count):
        attend_ending = (attend_index + 1) * block_rows
        rows_here = q_block[attend_index * block_rows : attend_ending]
        logits = (
            jnp.einsum(
                "thd,uhd->htu",
                rows_here,
                k_block[:attend_ending],
                preferred_element_type=jnp.float32,
            )
            * inv_root
        )
        causal = (attend_index * block_rows + lax.iota(jnp.int32, block_rows))[:, None] >= lax.iota(
            jnp.int32, attend_ending
        )[None, :]
        powers = jnp.where(causal[None], jnp.exp(logits), 0.0)
        stored.append(
            lax.optimization_barrier(
                (powers / jnp.sum(powers, axis=2, keepdims=True)).astype(jnp.bfloat16)
            )
        )
    blocks = stored
    saved_blocks = [blocks]
    live_len = pass_lens[passage]
    live_mask = (positions < live_len).astype(jnp.bfloat16)
    col_weight = jnp.zeros((local_heads, PASS_LEN), jnp.float32)
    for index in range(block_count):
        ending = (index + 1) * block_rows
        column_part = jnp.einsum(
            "t,htu->hu",
            live_mask[index * block_rows : ending],
            blocks[index],
            preferred_element_type=jnp.float32,
        )
        col_weight = col_weight.at[:, :ending].add(column_part)
    col_weight = col_weight / live_len.astype(jnp.float32)
    pooled_list = [jnp.sum(col_weight.T[:, :, None] * v_all[passage].astype(jnp.float32), axis=0)]
    weight_list = [col_weight.astype(jnp.bfloat16)]
    pooled = jnp.stack(pooled_list)
    col_weights = jnp.stack(weight_list)
    pooled_flat = pooled.reshape(passes, local_heads * HD).astype(jnp.bfloat16)
    partial_value = jnp.dot(pooled_flat, out_weight, preferred_element_type=jnp.float32)
    summed = lax.psum(partial_value, "seq")
    inv_norm = lax.rsqrt(jnp.sum(summed * summed, axis=1, keepdims=True) + 1e-06)
    passage_unit = summed * inv_norm
    passage_all = lax.all_gather(
        passage_unit.astype(jnp.bfloat16), ("blk", "rep"), axis=0, tiled=True
    )
    query_wide = query_emb.astype(jnp.float32)
    request_unit_length = (
        query_wide * lax.rsqrt(jnp.sum(query_wide * query_wide, axis=1, keepdims=True) + 1e-06)
    ).astype(jnp.bfloat16)
    learner_similarities = (
        lax.dot_general(
            request_unit_length,
            passage_all,
            (((1,), (1,)), ((), ())),
            preferred_element_type=jnp.float32,
        )
        / logit_divisor
    )
    exp_student = jnp.exp(learner_similarities)
    exp_teacher = jnp.exp(teacher)
    row_student = jnp.sum(exp_student, axis=1, keepdims=True)
    row_teacher = jnp.sum(exp_teacher, axis=1, keepdims=True)
    gap = exp_teacher * (teacher - learner_similarities)
    col_student, col_teacher, col_gap = lax.psum(
        (jnp.sum(exp_student, axis=0), jnp.sum(exp_teacher, axis=0), jnp.sum(gap, axis=0)), "blk"
    )
    row_loss = (
        jnp.sum(gap, axis=1) / row_teacher[:, 0]
        - jnp.log(row_teacher[:, 0])
        + jnp.log(row_student[:, 0])
    )
    col_loss = col_gap / col_teacher - jnp.log(col_teacher) + jnp.log(col_student)
    query_total = query_emb.shape[0] * blk_count
    passage_total = teacher.shape[1]
    similarity_derivative = (
        (exp_student / row_student - exp_teacher / row_teacher) / query_total
        + (exp_student / col_student - exp_teacher / col_teacher) / passage_total
    ).astype(jnp.bfloat16)
    grad_block = lax.psum_scatter(
        (
            lax.dot_general(
                similarity_derivative,
                request_unit_length,
                (((0,), (0,)), ((), ())),
                preferred_element_type=jnp.float32,
            )
            / logit_divisor
        ).astype(jnp.bfloat16),
        "blk",
        scatter_dimension=0,
        tiled=True,
    ).astype(jnp.float32)
    representation_derivative = lax.dynamic_slice_in_dim(
        grad_block, lax.axis_index("rep") * passes, passes, 0
    )
    grad_sum = (
        (
            representation_derivative
            - passage_unit
            * jnp.sum(passage_unit * representation_derivative, axis=1, keepdims=True)
        )
        * inv_norm
    ).astype(jnp.bfloat16)
    pooled_every, grads_every = (
        lax.all_gather(pooled_flat, ("blk", "rep"), axis=0, tiled=True),
        lax.all_gather(grad_sum, ("blk", "rep"), axis=0, tiled=True),
    )
    weight_grad = lax.dot_general(
        pooled_every, grads_every, (((0,), (0,)), ((), ())), preferred_element_type=jnp.float32
    ).astype(jnp.bfloat16)
    grad_pool = lax.dot_general(
        grad_sum, out_weight, (((1,), (1,)), ((), ())), preferred_element_type=jnp.float32
    )
    pool_heads = grad_pool.reshape(passes, local_heads, HD)
    passage = 0
    blocks = saved_blocks[passage]
    q_block = q_unit[passage]
    k_block = k_unit[passage]
    live_len = pass_lens[passage]
    live_mask = (positions < live_len).astype(jnp.float32) / live_len.astype(jnp.float32)
    value_dot = jnp.sum(v_all[passage].astype(jnp.float32) * pool_heads[passage][None], axis=2).T
    grad_k_copy = jnp.zeros((PASS_LEN, local_heads, HD), jnp.float32)
    query_parts = []
    for index in range(block_count):
        ending = (index + 1) * block_rows
        stored_block = blocks[index]
        value_here = value_dot[:, None, :ending]
        mean_dot = jnp.sum(stored_block.astype(jnp.float32) * value_here, axis=2)
        local_live_mask = live_mask[index * block_rows : ending]
        grad_logits = (
            stored_block.astype(jnp.float32)
            * local_live_mask[None, :, None]
            * (value_here - mean_dot[:, :, None])
            * inv_root
        ).astype(jnp.bfloat16)
        query_parts.append(
            jnp.einsum(
                "htu,uhd->thd", grad_logits, k_block[:ending], preferred_element_type=jnp.float32
            )
        )
        key_part = jnp.einsum(
            "htu,thd->uhd",
            grad_logits,
            q_block[index * block_rows : ending],
            preferred_element_type=jnp.float32,
        )
        grad_k_copy = grad_k_copy.at[:ending].add(key_part)
    grad_q_unit = jnp.concatenate(query_parts, axis=0)
    q_list = [norm_back(q_raw[passage], q_gain, grad_q_unit)]
    k_list = [norm_back(k_raw[passage], k_gain, grad_k_copy)]
    q_terms = jnp.stack(q_list)
    k_terms = jnp.stack(k_list)
    flat_shape = (group_tok, local_heads * HD)

    def narrow(terms):
        wide = terms.astype(jnp.float32).reshape(tok_dev, kv_heads, group_size, HD)
        return jnp.sum(wide, axis=2).astype(jnp.bfloat16).reshape(tok_dev, kv_heads * HD)

    q_back, k_back, v_back = (
        lax.all_to_all(q_terms.reshape(flat_shape), "seq", split_axis=0, concat_axis=1, tiled=True),
        lax.all_to_all(k_terms.reshape(flat_shape), "seq", split_axis=0, concat_axis=1, tiled=True),
        lax.all_to_all(
            (col_weights.astype(jnp.float32).transpose(0, 2, 1)[..., None] * pool_heads[:, None])
            .astype(jnp.bfloat16)
            .reshape(flat_shape),
            "seq",
            split_axis=0,
            concat_axis=1,
            tiled=True,
        ),
    )
    k_out = narrow(k_back)
    v_out = narrow(v_back)
    return (q_back[None], k_out[None], v_out[None], weight_grad, row_loss, col_loss)


def solution(mesh):
    placed = (
        P(("grp", "blk", "rep"), "seq", None),
        P(("grp", "blk", "rep"), "seq", None),
        P(("grp", "blk", "rep"), "seq", None),
        P(),
        P(),
        P("seq", None),
        P(("grp", "blk", "rep"), None),
        P(("grp", "blk"), None),
        P(("grp", "blk"), None),
    )
    return jax.shard_map(
        shards,
        mesh=mesh,
        in_specs=placed,
        out_specs=(
            P(("grp", "blk", "rep"), "seq", None),
            P(("grp", "blk", "rep"), "seq", None),
            P(("grp", "blk", "rep"), "seq", None),
            P(("grp", "seq"), None),
            P(("grp", "blk")),
            P("grp"),
        ),
        check_vma=False,
    )
```

profile of v0, /device:TPU:0, one launch (start us, length us, event | category | flops | bytes accessed | tf_op | source)
XLA Modules:
  0.0 180.6 jit_solution(1321558911935933446)
XLA Ops:
  0.7 1.1 copy.44
  1.8 0.8 broadcast_in_dim.25
  2.7 6.3 %all-to-all-start.1 = ((bf16[512,4,128]{0,2,1:T(8,128)(2,1)}), bf16[512,4,128]{0,2,1:T(8,128)(2,1)S(1)}, u32[]{:S(2)}, u32[]{:S(2)}) async-start(bf16[512,4,128]{0,2,1:T(8,128)(2,1)} %broadcast_in_dim.25), calls=%async_computation.1 | async-start | bytes 1048576 | tf_op jit(solution)/shard_map/all_to_all | solution.py:54
  9.0 1.0 copy.42
  10.7 12.7 %all-to-all-done.1 = bf16[512,4,128]{0,2,1:T(8,128)(2,1)S(1)} async-done(((bf16[512,4,128]{0,2,1:T(8,128)(2,1)}), bf16[512,4,128]{0,2,1:T(8,128)(2,1)S(1)}, u32[]{:S(2)}, u32[]{:S(2)}) %all-to-all-start.1) | async-done | bytes 524320 | tf_op jit(solution)/shard_map/all_to_all | solution.py:54
  23.5 3.5 %all-to-all-start = ((bf16[512,4,128]{0,2,1:T(8,128)(2,1)}), bf16[512,4,128]{0,2,1:T(8,128)(2,1)S(1)}, u32[]{:S(2)}, u32[]{:S(2)}) async-start(bf16[512,4,128]{0,2,1:T(8,128)(2,1)} %bitcast), calls=%async_computation | async-start | bytes 1048576 | tf_op jit(solution)/shard_map/all_to_all | solution.py:53
  31.1 9.8 %all-to-all-done = bf16[512,4,128]{0,2,1:T(8,128)(2,1)S(1)} async-done(((bf16[512,4,128]{0,2,1:T(8,128)(2,1)}), bf16[512,4,128]{0,2,1:T(8,128)(2,1)S(1)}, u32[]{:S(2)}, u32[]{:S(2)}) %all-to-all-start) | async-done | bytes 524320 | tf_op jit(solution)/shard_map/all_to_all | solution.py:53
  40.9 0.9 broadcast_in_dim.29
  41.8 4.3 %all-to-all-start.2 = ((bf16[512,4,128]{2,0,1:T(8,128)(2,1)}), bf16[512,4,128]{2,0,1:T(8,128)(2,1)}, u32[]{:S(2)}, u32[]{:S(2)}) async-start(bf16[512,4,128]{2,0,1:T(8,128)(2,1)} %broadcast_in_dim.29), calls=%async_computation.2 | async-start | bytes 1048576 | tf_op jit(solution)/shard_map/all_to_all | solution.py:55
  47.9 1.4 fusion.96
  52.5 1.0 fusion.99
  54.9 0.9 fusion.35
  55.8 1.0 fusion.16
  56.8 1.0 convert_reduce_fusion
  57.8 2.3 %all-to-all-done.2 = bf16[512,4,128]{2,0,1:T(8,128)(2,1)} async-done(((bf16[512,4,128]{2,0,1:T(8,128)(2,1)}), bf16[512,4,128]{2,0,1:T(8,128)(2,1)}, u32[]{:S(2)}, u32[]{:S(2)}) %all-to-all-start.2) | async-done | bytes 524320 | tf_op jit(solution)/shard_map/all_to_all | solution.py:55
  60.1 1.1 convert_element_type.407
  61.2 1.0 copy-done.11
  63.3 16.8 %psum.28 = f32[1,2560]{1,0:T(1,128)S(1)} all-reduce(f32[1,2560]{1,0:T(1,128)S(1)} %fusion.77), channel_id=1, replica_groups=mesh['grp'=2,'seq'=4,'blk'=2,'rep'=2] {'seq'}, use_global_device_ids=true, to_apply=%region_11.12 | all-reduce | flops 2560 | bytes 20480 | tf_op jit(solution)/shard_map/psum | solution.py:110
  81.4 5.2 %all-gather.1 = bf16[4,1,2560]{2,1,0:T(2,128)(2,1)S(1)} all-gather(bf16[1,1,2560]{2,1,0:T(2,128)(2,1)S(1)} %convert_bitcast_fusion.1), channel_id=1, replica_groups=mesh['grp'=2,'seq'=4,'blk'=2,'rep'=2] {'blk','rep'}, dimensions={0}, use_global_device_ids=true | all-gather | bytes 25600 | tf_op jit(solution)/shard_map/all_gather | solution.py:113
  86.6 2.0 %fusion.80 = (f32[4]{0:T(128)S(1)}, f32[128]{0:T(128)}, f32[4]{0:T(128)S(1)}, f32[128]{0:T(128)S(1)}, f32[4]{0:T(128)S(1)}, /*index=5*/f32[128]{0:T(128)S(1)}, f32[128,4]{0,1:T(4,128)S(1)}) fusion(f32[128,4]{0,1:T(4,128)S(1)} %copy-done.55, bf16[4,1,2560]{2,1,0:T(2,128)(2,1)S(1)} %all-gather.1, bf16[128,2560]{1,0:T(8,128)(2,1)} %param.36, ...), kind=kOutput, calls=%fused_computation.165 | convolution fusion | flops 3608692 | bytes 682032 | tf_op jit(solution)/shard_map/dot_general | solution.py:121
  88.6 5.4 %all-reduce.3 = (f32[4]{0:T(128)S(1)}, f32[4]{0:T(128)S(1)}, f32[4]{0:T(128)}) all-reduce(f32[4]{0:T(128)S(1)} %get-tuple-element.140, f32[4]{0:T(128)S(1)} %get-tuple-element.138, f32[4]{0:T(128)S(1)} %get-tuple-element.136), channel_id=1, replica_groups=mesh['grp'=2,'seq'=4,'blk'=2,'rep'=2] {'blk'}, use_global_device_ids=true, to_apply=%region_18.19 | all-reduce | flops 12 | bytes 96 | tf_op jit(solution)/shard_map/psum | solution.py:134
  94.1 1.4 fusion.4
  95.5 8.3 %all-reduce.2 = bf16[4,2560]{1,0:T(4,128)(2,1)S(1)} all-reduce(bf16[4,2560]{1,0:T(4,128)(2,1)S(1)} %fusion.4), channel_id=3, replica_groups=mesh['grp'=2,'seq'=4,'blk'=2,'rep'=2] {'blk'}, use_global_device_ids=true, to_apply=%region_19.20.clone | all-reduce | flops 10240 | bytes 40960
  105.9 1.6 fusion.44
  108.6 2.1 %convolution_bitcast_fusion.3 = f32[512,1,128]{0,2,1:T(8,128)} fusion(bf16[1,2048,1,128]{3,1,2,0:T(8,128)(2,1)} %copy-done.19, bf16[1,512,512]{1,2,0:T(8,128)(2,1)S(1)} %fusion.55, f32[512]{0:T(512)S(1)} %fusion.39, f32[512]{0:T(512)S(1)} %bitcast.270, f32[512]{0:T(512)S(1)} %get-tuple-element.148), kind=kOutput, calls=%fused_computation.61 | convolution fusion | flops 68681728 | bytes 923648 | tf_op jit(solution)/shard_map/htu,thd->uhd/dot_general | solution.py:211
  112.0 1.3 fusion.87
  113.3 0.9 copy-done.8
  114.9 0.9 fusion.56
  117.3 1.1 pad_maximum_fusion
  118.4 2.5 %copy.54 = f32[2048,128]{1,0:T(8,128)} copy(f32[2048,128]{0,1:T(8,128)} %pad_maximum_fusion) | data formatting | bytes 2097152 | tf_op jit(solution)/shard_map/concatenate | solution.py:218
  120.9 1.3 copy.55
  122.3 1.6 fusion.42
  123.9 2.9 %fusion.49 = bf16[4,512,128]{2,1,0:T(8,128)(2,1)} fusion(f32[4,512,128]{2,1,0:T(8,128)} %bitcast.241, bf16[512,4,128]{2,0,1:T(8,128)(2,1)} %copy-done.15, f32[4,512]{1,0:T(4,128)S(1)} %div.160, f32[4,512]{1,0:T(4,128)} %get-tuple-element.147, f32[128]{0:T(128)} %param.32, f32[4,512]{1,0:T(4,128)} %get-tuple-element.145), kind=kLoop, calls=%fused_computation.86 | loop fusion | flops 1835008 | bytes 2122240 | tf_op jit(solution)/shard_map/convert_element_type | solution.py:28
  126.8 2.1 %copy.48 = bf16[4,512,128]{1,2,0:T(8,128)(2,1)} copy(bf16[4,512,128]{2,1,0:T(8,128)(2,1)} %fusion.49) | data formatting | bytes 1048576 | tf_op jit(solution)/shard_map/convert_element_type | solution.py:28
  128.9 4.1 %all-to-all-start.3 = ((bf16[4,512,128]{1,2,0:T(8,128)(2,1)}), bf16[4,512,128]{1,2,0:T(8,128)(2,1)}, u32[]{:S(2)}, u32[]{:S(2)}) async-start(bf16[4,512,128]{1,2,0:T(8,128)(2,1)} %copy.48), calls=%async_computation.3 | async-start | bytes 1048576 | tf_op jit(solution)/shard_map/all_to_all | solution.py:230
  133.1 1.3 copy.56
  134.5 2.0 %fusion.33 = f32[2048,1,128]{0,2,1:T(8,128)S(1)} fusion(f32[2048,1,128]{0,2,1:T(8,128)S(1)} %scatter-add.25, bf16[1,2048,1,128]{3,1,2,0:T(8,128)(2,1)} %copy-done.19, bf16[1,512,1024]{2,1,0:T(8,128)(2,1)} %copy-done.12, f32[512]{0:T(512)} %copy-done.41, f32[1024]{0:T(1024)} %bitcast.267, f32[512]{0:T(512)} %get-tuple-element.151), kind=kOutput, calls=%fused_computation.60 | convolution fusion | flops 137494528 | bytes 2236416 | tf_op jit(solution)/shard_map/htu,thd->uhd/dot_general | solution.py:211
  136.5 0.9 fusion.12
  139.6 0.9 copy.50
  140.5 4.7 %all-to-all-done.3 = bf16[4,512,128]{1,2,0:T(8,128)(2,1)} async-done(((bf16[4,512,128]{1,2,0:T(8,128)(2,1)}), bf16[4,512,128]{1,2,0:T(8,128)(2,1)}, u32[]{:S(2)}, u32[]{:S(2)}) %all-to-all-start.3) | async-done | bytes 524320 | tf_op jit(solution)/shard_map/all_to_all | solution.py:230
  145.2 3.5 %all-to-all-start.4 = ((bf16[4,512,128]{1,2,0:T(8,128)(2,1)}), bf16[4,512,128]{1,2,0:T(8,128)(2,1)S(1)}, u32[]{:S(2)}, u32[]{:S(2)}) async-start(bf16[4,512,128]{1,2,0:T(8,128)(2,1)} %copy.50), calls=%async_computation.4 | async-start | bytes 1048576 | tf_op jit(solution)/shard_map/all_to_all | solution.py:231
  148.7 1.1 multiply_convert_fusion
  149.8 11.1 %all-to-all-done.4 = bf16[4,512,128]{1,2,0:T(8,128)(2,1)S(1)} async-done(((bf16[4,512,128]{1,2,0:T(8,128)(2,1)}), bf16[4,512,128]{1,2,0:T(8,128)(2,1)S(1)}, u32[]{:S(2)}, u32[]{:S(2)}) %all-to-all-start.4) | async-done | bytes 524320 | tf_op jit(solution)/shard_map/all_to_all | solution.py:231
  160.9 3.5 %all-to-all-start.5 = ((bf16[4,512,128]{2,1,0:T(8,128)(2,1)}), bf16[4,512,128]{2,1,0:T(8,128)(2,1)S(1)}, u32[]{:S(2)}, u32[]{:S(2)}) async-start(bf16[4,512,128]{2,1,0:T(8,128)(2,1)} %multiply_convert_fusion), calls=%async_computation.5 | async-start | bytes 1048576 | tf_op jit(solution)/shard_map/all_to_all | solution.py:232
  164.4 5.0 %all-gather.2 = bf16[4,1,128]{2,1,0:T(2,128)(2,1)S(1)} all-gather(bf16[1,1,128]{2,1,0:T(2,128)(2,1)S(1)} %bitcast.273), channel_id=2, replica_groups=mesh['grp'=2,'seq'=4,'blk'=2,'rep'=2] {'blk','rep'}, dimensions={0}, use_global_device_ids=true | all-gather | bytes 1280 | tf_op jit(solution)/shard_map/all_gather | solution.py:175
  169.4 5.2 %all-gather.3 = bf16[4,1,2560]{2,1,0:T(2,128)(2,1)S(1)} all-gather(bf16[1,1,2560]{2,1,0:T(2,128)(2,1)S(1)} %bitcast.262), channel_id=1, replica_groups=mesh['grp'=2,'seq'=4,'blk'=2,'rep'=2] {'blk','rep'}, dimensions={0}, use_global_device_ids=true | all-gather | bytes 25600 | tf_op jit(solution)/shard_map/all_gather | solution.py:176
  175.7 1.2 convolution_convert_fusion
  176.9 2.0 %copy.52 = bf16[1,512,512]{2,1,0:T(8,128)(2,1)} copy(bf16[1,512,512]{1,2,0:T(8,128)(2,1)} %bitcast.63) | data formatting | bytes 1048576
  (181 shorter events, 22.8 us)
Async XLA Ops:
  0.6 62.5 %copy-start = (bf16[128,2560]{1,0:T(8,128)(2,1)S(1)}, bf16[128,2560]{1,0:T(8,128)(2,1)}, u32[]{:S(2)}) copy-start(bf16[128,2560]{1,0:T(8,128)(2,1)} %param.34) | copy-start | bytes 1966084
  0.6 26.4 %copy-start.56 = (u32[32]{0:T(128)S(1)}, u32[32]{0:T(128)}, u32[]{:S(2)}) copy-start(u32[32]{0:T(128)} %constant.272) | copy-start | bytes 388
  0.7 8.3 %copy-start.22 = (bf16[1,512,512]{2,1,0:T(8,128)(2,1)S(1)}, bf16[1,512,512]{2,1,0:T(8,128)(2,1)}, u32[]{:S(2)}) copy-start(bf16[1,512,512]{2,1,0:T(8,128)(2,1)} %param.29) | copy-start | bytes 1572868
  0.7 28.9 %copy-start.21 = (bf16[128,2560]{1,0:T(8,128)(2,1)S(1)}, bf16[128,2560]{1,0:T(8,128)(2,1)}, u32[]{:S(2)}) copy-start(bf16[128,2560]{1,0:T(8,128)(2,1)} %param.36) | copy-start | bytes 1966084
  2.7 20.8 %all-to-all-start.1 = ((bf16[512,4,128]{0,2,1:T(8,128)(2,1)}), bf16[512,4,128]{0,2,1:T(8,128)(2,1)S(1)}, u32[]{:S(2)}, u32[]{:S(2)}) async-start(bf16[512,4,128]{0,2,1:T(8,128)(2,1)} %broadcast_in_dim.25), calls=%async_computation.1 | async-start | bytes 1048576 | tf_op jit(solution)/shard_map/all_to_all | solution.py:54
  23.5 17.4 %all-to-all-start = ((bf16[512,4,128]{0,2,1:T(8,128)(2,1)}), bf16[512,4,128]{0,2,1:T(8,128)(2,1)S(1)}, u32[]{:S(2)}, u32[]{:S(2)}) async-start(bf16[512,4,128]{0,2,1:T(8,128)(2,1)} %bitcast), calls=%async_computation | async-start | bytes 1048576 | tf_op jit(solution)/shard_map/all_to_all | solution.py:53
  26.9 14.0 %copy-start.26 = (bf16[1,512,128]{2,1,0:T(8,128)(2,1)S(1)}, bf16[1,512,128]{2,1,0:T(8,128)(2,1)}, u32[]{:S(2)}) copy-start(bf16[1,512,128]{2,1,0:T(8,128)(2,1)} %param.31) | copy-start | bytes 393220
  30.7 17.1 %copy-start.3 = (f32[512,4,128]{2,0,1:T(8,128)}, f32[512,4,128]{2,0,1:T(8,128)S(1)}, u32[]{:S(2)}) copy-start(f32[512,4,128]{2,0,1:T(8,128)S(1)} %convert_element_type.405) | copy-start | bytes 3145732
  41.8 5.8 %copy-start.31 = (f32[128]{0:T(128)S(1)}, f32[128]{0:T(128)}, u32[]{:S(2)}) copy-start(f32[128]{0:T(128)} %param.32) | copy-start | bytes 1540
  41.8 18.3 %all-to-all-start.2 = ((bf16[512,4,128]{2,0,1:T(8,128)(2,1)}), bf16[512,4,128]{2,0,1:T(8,128)(2,1)}, u32[]{:S(2)}, u32[]{:S(2)}) async-start(bf16[512,4,128]{2,0,1:T(8,128)(2,1)} %broadcast_in_dim.29), calls=%async_computation.2 | async-start | bytes 1048576 | tf_op jit(solution)/shard_map/all_to_all | solution.py:55
  46.3 3.0 %copy-start.15 = (bf16[512,4,128]{2,0,1:T(8,128)(2,1)}, bf16[512,4,128]{2,0,1:T(8,128)(2,1)S(1)}, u32[]{:S(2)}) copy-start(bf16[512,4,128]{2,0,1:T(8,128)(2,1)S(1)} %copy.43) | copy-start | bytes 1572868
  47.9 4.5 %copy-start.19 = (bf16[1,2048,1,128]{3,1,2,0:T(8,128)(2,1)}, bf16[1,2048,1,128]{3,1,2,0:T(8,128)(2,1)S(1)}, u32[]{:S(2)}) copy-start(bf16[1,2048,1,128]{3,1,2,0:T(8,128)(2,1)S(1)} %multiply_convert_fusion.2) | copy-start | bytes 1572868
  52.4 2.4 %copy-start.12 = (bf16[1,512,1024]{2,1,0:T(8,128)(2,1)}, bf16[1,512,1024]{2,1,0:T(8,128)(2,1)S(1)}, u32[]{:S(2)}) copy-start(bf16[1,512,1024]{2,1,0:T(8,128)(2,1)S(1)} %fusion.50) | copy-start | bytes 3145732
  53.9 1.9 %copy-start.7 = (bf16[1,512,1536]{2,1,0:T(8,128)(2,1)}, bf16[1,512,1536]{2,1,0:T(8,128)(2,1)S(1)}, u32[]{:S(2)}) copy-start(bf16[1,512,1536]{2,1,0:T(8,128)(2,1)S(1)} %fusion.27) | copy-start | bytes 4718596
  57.8 28.9 %copy-start.55 = (f32[128,4]{0,1:T(4,128)S(1)}, f32[128,4]{0,1:T(4,128)}, u32[]{:S(2)}) copy-start(f32[128,4]{0,1:T(4,128)} %param.37) | copy-start | bytes 6148
  88.6 19.3 %copy-start.46 = (f32[128]{0:T(128)}, f32[128]{0:T(128)S(1)}, u32[]{:S(2)}) copy-start(f32[128]{0:T(128)S(1)} %get-tuple-element.139) | copy-start | bytes 1540
  88.6 19.3 %copy-start.48 = (f32[128]{0:T(128)}, f32[128]{0:T(128)S(1)}, u32[]{:S(2)}) copy-start(f32[128]{0:T(128)S(1)} %get-tuple-element.141) | copy-start | bytes 1540
  94.1 9.7 %copy-start.50 = (f32[4]{0:T(128)}, f32[4]{0:T(128)S(1)}, u32[]{:S(2)}) copy-start(f32[4]{0:T(128)S(1)} %get-tuple-element.142) | copy-start | bytes 52
  94.1 9.7 %copy-start.52 = (f32[4]{0:T(128)}, f32[4]{0:T(128)S(1)}, u32[]{:S(2)}) copy-start(f32[4]{0:T(128)S(1)} %get-tuple-element.143) | copy-start | bytes 52
  105.0 3.1 %copy-start.27 = (bf16[1,2560]{1,0:T(2,128)(2,1)}, bf16[1,2560]{1,0:T(2,128)(2,1)S(1)}, u32[]{:S(2)}) copy-start(bf16[1,2560]{1,0:T(2,128)(2,1)S(1)} %subtract_multiply_fusion) | copy-start | bytes 15364
  105.1 3.1 %copy-start.24 = (bf16[1,2048,1,128]{3,1,2,0:T(8,128)(2,1)S(1)}, bf16[1,2048,1,128]{3,1,2,0:T(8,128)(2,1)}, u32[]{:S(2)}) copy-start(bf16[1,2048,1,128]{3,1,2,0:T(8,128)(2,1)} %copy-done.23) | copy-start | bytes 1572868
  108.0 7.9 %copy-start.30 = (f32[1,1024]{1,0:T(1,128)}, f32[1,1024]{1,0:T(1,128)S(1)}, u32[]{:S(2)}) copy-start(f32[1,1024]{1,0:T(1,128)S(1)} %slice.261) | copy-start | bytes 12292
  108.6 7.9 %copy-start.16 = (f32[128,512]{1,0:T(8,128)}, f32[128,512]{1,0:T(8,128)S(1)}, u32[]{:S(2)}) copy-start(f32[128,512]{1,0:T(8,128)S(1)} %fusion.60) | copy-start | bytes 786436
  112.0 2.6 %copy-start.1 = (bf16[512,2048]{1,0:T(8,128)(2,1)}, bf16[512,2048]{1,0:T(8,128)(2,1)S(1)}, u32[]{:S(2)}) copy-start(bf16[512,2048]{1,0:T(8,128)(2,1)S(1)} %fusion.22) | copy-start | bytes 6291460
  112.0 2.2 %copy-start.8 = (bf16[1,512,1536]{2,1,0:T(8,128)(2,1)S(1)}, bf16[1,512,1536]{2,1,0:T(8,128)(2,1)}, u32[]{:S(2)}) copy-start(bf16[1,512,1536]{2,1,0:T(8,128)(2,1)} %copy-done.7) | copy-start | bytes 4718596
  112.0 2.6 %copy-start.13 = (bf16[1,512,1024]{2,1,0:T(8,128)(2,1)S(1)}, bf16[1,512,1024]{2,1,0:T(8,128)(2,1)}, u32[]{:S(2)}) copy-start(bf16[1,512,1024]{2,1,0:T(8,128)(2,1)} %copy-done.12) | copy-start | bytes 3145732
  117.3 3.7 %copy-start.10 = (f32[512,4,128]{2,0,1:T(8,128)S(1)}, f32[512,4,128]{2,0,1:T(8,128)}, u32[]{:S(2)}) copy-start(f32[512,4,128]{2,0,1:T(8,128)} %copy-done.9) | copy-start | bytes 3145732
  123.9 9.2 %copy-start.6 = (f32[512,4,128]{2,0,1:T(8,128)S(1)}, f32[512,4,128]{2,0,1:T(8,128)}, u32[]{:S(2)}) copy-start(f32[512,4,128]{2,0,1:T(8,128)} %copy-done.3) | copy-start | bytes 3145732
  126.8 7.6 %copy-start.25 = (f32[512,1,128]{0,2,1:T(8,128)S(1)}, f32[512,1,128]{0,2,1:T(8,128)}, u32[]{:S(2)}) copy-start(f32[512,1,128]{0,2,1:T(8,128)} %convolution_bitcast_fusion.3) | copy-start | bytes 786436
  128.9 16.3 %all-to-all-start.3 = ((bf16[4,512,128]{1,2,0:T(8,128)(2,1)}), bf16[4,512,128]{1,2,0:T(8,128)(2,1)}, u32[]{:S(2)}, u32[]{:S(2)}) async-start(bf16[4,512,128]{1,2,0:T(8,128)(2,1)} %copy.48), calls=%async_computation.3 | async-start | bytes 1048576 | tf_op jit(solution)/shard_map/all_to_all | solution.py:230
  134.4 2.1 %copy-start.20 = (bf16[1,2048,1,128]{3,1,2,0:T(8,128)(2,1)S(1)}, bf16[1,2048,1,128]{3,1,2,0:T(8,128)(2,1)}, u32[]{:S(2)}) copy-start(bf16[1,2048,1,128]{3,1,2,0:T(8,128)(2,1)} %copy-done.19) | copy-start | bytes 1572868
  134.4 2.1 %copy-start.40 = (f32[512]{0:T(512)S(1)}, f32[512]{0:T(512)}, u32[]{:S(2)}) copy-start(f32[512]{0:T(512)} %copy-done.39) | copy-start | bytes 6148
  134.4 2.1 %copy-start.43 = (f32[512]{0:T(512)S(1)}, f32[512]{0:T(512)}, u32[]{:S(2)}) copy-start(f32[512]{0:T(512)} %get-tuple-element.150) | copy-start | bytes 6148
  136.5 1.6 copy-start.2
  136.5 1.8 %copy-start.14 = (f32[2048,1,128]{0,2,1:T(8,128)S(1)}, f32[2048,1,128]{0,2,1:T(8,128)}, u32[]{:S(2)}) copy-start(f32[2048,1,128]{0,2,1:T(8,128)} %copy.56) | copy-start | bytes 3145732
  136.5 1.8 %copy-start.34 = (f32[128]{0:T(128)S(1)}, f32[128]{0:T(128)}, u32[]{:S(2)}) copy-start(f32[128]{0:T(128)} %param.33) | copy-start | bytes 1540
  139.1 9.6 %copy-start.29 = (f32[2048]{0:T(1024)S(1)}, f32[2048]{0:T(1024)}, u32[]{:S(2)}) copy-start(f32[2048]{0:T(1024)} %get-tuple-element.167) | copy-start | bytes 24580
  139.1 9.6 %copy-start.36 = (f32[128]{0:T(128)S(1)}, f32[128]{0:T(128)}, u32[]{:S(2)}) copy-start(f32[128]{0:T(128)} %copy-done.35) | copy-start | bytes 1540
  139.5 24.9 %copy-start.38 = (bf16[128]{0:T(256)(128)(2,1)S(1)}, bf16[128]{0:T(256)(128)(2,1)}, u32[]{:S(2)}) copy-start(bf16[128]{0:T(256)(128)(2,1)} %copy-done.37) | copy-start | bytes 772
  139.5 29.9 %copy-start.28 = (bf16[1,2560]{1,0:T(2,128)(2,1)S(1)}, bf16[1,2560]{1,0:T(2,128)(2,1)}, u32[]{:S(2)}) copy-start(bf16[1,2560]{1,0:T(2,128)(2,1)} %copy-done.27) | copy-start | bytes 15364
  139.5 35.1 %copy-start.45 = (f32[128]{0:T(128)S(1)}, f32[128]{0:T(128)}, u32[]{:S(2)}) copy-start(f32[128]{0:T(128)} %get-tuple-element.137) | copy-start | bytes 1540
  139.6 35.1 %copy-start.47 = (f32[128]{0:T(128)S(1)}, f32[128]{0:T(128)}, u32[]{:S(2)}) copy-start(f32[128]{0:T(128)} %copy-done.46) | copy-start | bytes 1540
  139.6 35.1 %copy-start.49 = (f32[128]{0:T(128)S(1)}, f32[128]{0:T(128)}, u32[]{:S(2)}) copy-start(f32[128]{0:T(128)} %copy-done.48) | copy-start | bytes 1540
  139.6 35.6 %copy-start.51 = (f32[4]{0:T(128)S(1)}, f32[4]{0:T(128)}, u32[]{:S(2)}) copy-start(f32[4]{0:T(128)} %copy-done.50) | copy-start | bytes 52
  139.6 35.6 %copy-start.53 = (f32[4]{0:T(128)S(1)}, f32[4]{0:T(128)}, u32[]{:S(2)}) copy-start(f32[4]{0:T(128)} %copy-done.52) | copy-start | bytes 52
  139.6 35.6 %copy-start.54 = (f32[4]{0:T(128)S(1)}, f32[4]{0:T(128)}, u32[]{:S(2)}) copy-start(f32[4]{0:T(128)} %get-tuple-element.144) | copy-start | bytes 52
  145.2 15.7 %all-to-all-start.4 = ((bf16[4,512,128]{1,2,0:T(8,128)(2,1)}), bf16[4,512,128]{1,2,0:T(8,128)(2,1)S(1)}, u32[]{:S(2)}, u32[]{:S(2)}) async-start(bf16[4,512,128]{1,2,0:T(8,128)(2,1)} %copy.50), calls=%async_computation.4 | async-start | bytes 1048576 | tf_op jit(solution)/shard_map/all_to_all | solution.py:231
  160.9 18.9 %all-to-all-start.5 = ((bf16[4,512,128]{2,1,0:T(8,128)(2,1)}), bf16[4,512,128]{2,1,0:T(8,128)(2,1)S(1)}, u32[]{:S(2)}, u32[]{:S(2)}) async-start(bf16[4,512,128]{2,1,0:T(8,128)(2,1)} %multiply_convert_fusion), calls=%async_computation.5 | async-start | bytes 1048576 | tf_op jit(solution)/shard_map/all_to_all | solution.py:232
  (15 other events, 15.4 us)
where the time goes:
time: 182 us; the launch traced here: 181 us
  blocking collectives  46 us (25%)
  waiting for transfers between devices  40.6 us (22%)
  starting transfers between devices  25.1 us (14%)
  local copies, waits for them, and re-layouts  23 us (13%)
  other arithmetic  21.8 us (12%)
  matrix products  20.4 us (11%)
  between operations  3.64 us (2%)
    psum x1, blocking collectives, shards(): summed = lax.psum(partial_value, 'seq')  16.8 us
    all_to_all x1, waiting for transfers between devices, shards(): lax.all_to_all(widen(k_proj[0]), 'seq', split_axis=1, concat_axis=0, tile...  12.7 us
    all_to_all x1, waiting for transfers between devices, shards(): lax.all_to_all(k_terms.reshape(flat_shape), 'seq', split_axis=0, concat_a...  11.1 us
    unnamed x120, local copies, waits for them, and re-layouts  10.3 us
    all_to_all x1, waiting for transfers between devices, shards(): lax.all_to_all(q_proj[0], 'seq', split_axis=1, concat_axis=0, tiled=True)  9.79 us
    unnamed x1, blocking collectives  8.26 us
    all_to_all x1, starting transfers between devices, shards(): lax.all_to_all(widen(k_proj[0]), 'seq', split_axis=1, concat_axis=0, tile...  6.32 us
    dot_general x4, matrix products, shards(): jnp.einsum('htu,thd->uhd', grad_logits, q_block[index * block_rows:ending...  5.53 us
  transfers between devices with their start and end apart: 6, of which 5 were waited for; matrix products, arithmetic and copies ran while one was open for 15% of the time, Pallas kernels for 0%

commit v1 on v0

--- a/solution.py
+++ b/solution.py
@@ -3,10 +3,44 @@
 import jax.numpy as jnp
 from jax import lax
 from jax.sharding import PartitionSpec as P
+from jax.lax import axis_index, axis_size, ppermute
 
 HD = 128
 PASS_LEN = 2048
 logit_divisor = 0.05
+
+
+def manage_the_strips_all(buf, axis_no, arr_in):
+    a_next = buf.shape
+    v_next = buf.reshape(
+        *a_next[:axis_no], arr_in, a_next[axis_no] // arr_in, *a_next[axis_no + 1 :]
+    )
+    return jnp.moveaxis(v_next, axis_no, 0)
+
+
+def boxes_scan(piece_in, dimension_no):
+    piece_in = jnp.moveaxis(piece_in, 0, dimension_no)
+    extra = piece_in.shape
+    return piece_in.reshape(
+        *extra[:dimension_no],
+        extra[dimension_no] * extra[dimension_no + 1],
+        *extra[dimension_no + 2 :]
+    )
+
+
+def prepare_islands_on(array_in, dev_axis, x_local, local_block):
+    row_out = axis_size(dev_axis)
+    left_arr = axis_index(dev_axis)
+    parts_out, current_block = (row_out, left_arr)
+    response = manage_the_strips_all(array_in, x_local, parts_out)
+    grid = [response[current_block]]
+    for rr in range(1, parts_out):
+        mixed_arr = response[current_block ^ rr]
+        a_now = ppermute(mixed_arr, dev_axis, [(jj, jj ^ rr) for jj in range(parts_out)])
+        grid.append(a_now)
+    later = jnp.stack(grid, 0)
+    response = later[current_block ^ jnp.arange(parts_out)]
+    return boxes_scan(response, local_block)
 
 
 def rms_scale(wide):
@@ -228,7 +262,7 @@
 
     q_back, k_back, v_back = (
         lax.all_to_all(q_terms.reshape(flat_shape), "seq", split_axis=0, concat_axis=1, tiled=True),
-        lax.all_to_all(k_terms.reshape(flat_shape), "seq", split_axis=0, concat_axis=1, tiled=True),
+        prepare_islands_on(k_terms.reshape(flat_shape), "seq", 0, local_block=1),
         lax.all_to_all(
             (col_weights.astype(jnp.float32).transpose(0, 2, 1)[..., None] * pool_heads[:, None])
             .astype(jnp.bfloat16)

time: 182 us -> 178 us (0.978)
  waiting for transfers between devices: 40.6 us -> 33.3 us
  starting transfers between devices: 25.1 us -> 27.7 us
  other arithmetic: 21.8 us -> 23.8 us
    all_to_all x1 -> x0, waiting for transfers between devices: 11.1 us -> none  [shards(): lax.all_to_all(k_terms.reshape(flat_shape), 'seq', split_axis=0, concat_a...]
    all_to_all x1, waiting for transfers between devices: 0.01 us -> 9.04 us  [shards(): lax.all_to_all((col_weights.astype(jnp.float32).transpose(0, 2, 1)[..., N...]
    all_to_all x1, waiting for transfers between devices: 4.71 us -> 0.01 us  [shards(): lax.all_to_all(q_terms.reshape(flat_shape), 'seq', split_axis=0, concat_a...]
    ppermute x0 -> x3, starting transfers between devices: none -> 4.47 us  [prepare_islands_on(): ppermute(mixed_arr, dev_axis, [(jj, jj ^ rr) for jj in range(parts_out)])]
    all_to_all x1 -> x0, starting transfers between devices: 3.47 us -> none  [shards(): lax.all_to_all(k_terms.reshape(flat_shape), 'seq', split_axis=0, concat_a...]
    unnamed x120 -> x121, local copies, waits for them, and re-layouts: 10.3 us -> 9.67 us
  transfers between devices with their start and end apart: 6 -> 8, of which waited for: 5 -> 4; matrix products, arithmetic and copies ran while one was open for 15% -> 16% of each run, Pallas kernels for 0% -> 0%
where the time goes in v1:
time: 178 us; the launch traced here: 177 us
  blocking collectives  46 us (26%)
  waiting for transfers between devices  33.3 us (19%)
  starting transfers between devices  27.7 us (16%)
  other arithmetic  23.8 us (13%)
  local copies, waits for them, and re-layouts  22.2 us (12%)
  matrix products  20.4 us (11%)
  between operations  3.62 us (2%)
    psum x1, blocking collectives, shards(): summed = lax.psum(partial_value, 'seq')  16.8 us
    all_to_all x1, waiting for transfers between devices, shards(): lax.all_to_all(widen(k_proj[0]), 'seq', split_axis=1, concat_axis=0, tile...  12.1 us
    all_to_all x1, waiting for transfers between devices, shards(): lax.all_to_all(q_proj[0], 'seq', split_axis=1, concat_axis=0, tiled=True)  9.77 us
    unnamed x121, local copies, waits for them, and re-layouts  9.67 us
    all_to_all x1, waiting for transfers between devices, shards(): lax.all_to_all((col_weights.astype(jnp.float32).transpose(0, 2, 1)[..., N...  9.04 us
    unnamed x1, blocking collectives  8.26 us
    all_to_all x1, starting transfers between devices, shards(): lax.all_to_all(widen(k_proj[0]), 'seq', split_axis=1, concat_axis=0, tile...  6.32 us
    dot_general x4, matrix products, shards(): jnp.einsum('htu,thd->uhd', grad_logits, q_block[index * block_rows:ending...  5.54 us
  transfers between devices with their start and end apart: 8, of which 4 were waited for; matrix products, arithmetic and copies ran while one was open for 16% of the time, Pallas kernels for 0%

profile of v1, /device:TPU:0, one launch (start us, length us, event | category | flops | bytes accessed | tf_op | source)
XLA Modules:
  0.0 176.9 jit_solution(9903260493630148989)
XLA Ops:
  0.7 1.1 copy.50
  1.8 0.8 broadcast_in_dim.25
  2.7 6.3 %all-to-all-start.1 = ((bf16[512,4,128]{0,2,1:T(8,128)(2,1)}), bf16[512,4,128]{0,2,1:T(8,128)(2,1)S(1)}, u32[]{:S(2)}, u32[]{:S(2)}) async-start(bf16[512,4,128]{0,2,1:T(8,128)(2,1)} %broadcast_in_dim.25), calls=%async_computation.1 | async-start | bytes 1048576 | tf_op jit(solution)/shard_map/all_to_all | solution.py:88
  9.0 1.0 copy.48
  11.3 12.1 %all-to-all-done.1 = bf16[512,4,128]{0,2,1:T(8,128)(2,1)S(1)} async-done(((bf16[512,4,128]{0,2,1:T(8,128)(2,1)}), bf16[512,4,128]{0,2,1:T(8,128)(2,1)S(1)}, u32[]{:S(2)}, u32[]{:S(2)}) %all-to-all-start.1) | async-done | bytes 524320 | tf_op jit(solution)/shard_map/all_to_all | solution.py:88
  23.5 3.5 %all-to-all-start = ((bf16[512,4,128]{0,2,1:T(8,128)(2,1)}), bf16[512,4,128]{0,2,1:T(8,128)(2,1)S(1)}, u32[]{:S(2)}, u32[]{:S(2)}) async-start(bf16[512,4,128]{0,2,1:T(8,128)(2,1)} %bitcast), calls=%async_computation | async-start | bytes 1048576 | tf_op jit(solution)/shard_map/all_to_all | solution.py:87
  31.1 9.8 %all-to-all-done = bf16[512,4,128]{0,2,1:T(8,128)(2,1)S(1)} async-done(((bf16[512,4,128]{0,2,1:T(8,128)(2,1)}), bf16[512,4,128]{0,2,1:T(8,128)(2,1)S(1)}, u32[]{:S(2)}, u32[]{:S(2)}) %all-to-all-start) | async-done | bytes 524320 | tf_op jit(solution)/shard_map/all_to_all | solution.py:87
  40.9 0.9 broadcast_in_dim.29
  41.8 4.3 %all-to-all-start.2 = ((bf16[512,4,128]{2,0,1:T(8,128)(2,1)}), bf16[512,4,128]{2,0,1:T(8,128)(2,1)}, u32[]{:S(2)}, u32[]{:S(2)}) async-start(bf16[512,4,128]{2,0,1:T(8,128)(2,1)} %broadcast_in_dim.29), calls=%async_computation.2 | async-start | bytes 1048576 | tf_op jit(solution)/shard_map/all_to_all | solution.py:89
  47.9 1.4 fusion.97
  52.4 1.0 fusion.100
  54.8 0.9 fusion.35
  55.8 1.0 fusion.16
  56.7 1.0 convert_reduce_fusion
  57.7 2.4 %all-to-all-done.2 = bf16[512,4,128]{2,0,1:T(8,128)(2,1)} async-done(((bf16[512,4,128]{2,0,1:T(8,128)(2,1)}), bf16[512,4,128]{2,0,1:T(8,128)(2,1)}, u32[]{:S(2)}, u32[]{:S(2)}) %all-to-all-start.2) | async-done | bytes 524320 | tf_op jit(solution)/shard_map/all_to_all | solution.py:89
  60.1 1.1 convert_element_type.407
  61.2 1.0 copy-done.11
  63.3 16.8 %psum.28 = f32[1,2560]{1,0:T(1,128)S(1)} all-reduce(f32[1,2560]{1,0:T(1,128)S(1)} %fusion.78), channel_id=1, replica_groups=mesh['grp'=2,'seq'=4,'blk'=2,'rep'=2] {'seq'}, use_global_device_ids=true, to_apply=%region_11.12 | all-reduce | flops 2560 | bytes 20480 | tf_op jit(solution)/shard_map/psum | solution.py:144
  81.5 5.2 %all-gather.1 = bf16[4,1,2560]{2,1,0:T(2,128)(2,1)S(1)} all-gather(bf16[1,1,2560]{2,1,0:T(2,128)(2,1)S(1)} %convert_bitcast_fusion.1), channel_id=1, replica_groups=mesh['grp'=2,'seq'=4,'blk'=2,'rep'=2] {'blk','rep'}, dimensions={0}, use_global_device_ids=true | all-gather | bytes 25600 | tf_op jit(solution)/shard_map/all_gather | solution.py:147
  86.7 2.0 %fusion.81 = (f32[4]{0:T(128)S(1)}, f32[128]{0:T(128)}, f32[4]{0:T(128)S(1)}, f32[128]{0:T(128)S(1)}, f32[4]{0:T(128)S(1)}, /*index=5*/f32[128]{0:T(128)S(1)}, f32[128,4]{0,1:T(4,128)S(1)}) fusion(f32[128,4]{0,1:T(4,128)S(1)} %copy-done.56, bf16[4,1,2560]{2,1,0:T(2,128)(2,1)S(1)} %all-gather.1, bf16[128,2560]{1,0:T(8,128)(2,1)} %param.36, ...), kind=kOutput, calls=%fused_computation.174 | convolution fusion | flops 3608692 | bytes 682032 | tf_op jit(solution)/shard_map/dot_general | solution.py:155
  88.6 5.4 %all-reduce.3 = (f32[4]{0:T(128)S(1)}, f32[4]{0:T(128)S(1)}, f32[4]{0:T(128)}) all-reduce(f32[4]{0:T(128)S(1)} %get-tuple-element.140, f32[4]{0:T(128)S(1)} %get-tuple-element.138, f32[4]{0:T(128)S(1)} %get-tuple-element.136), channel_id=1, replica_groups=mesh['grp'=2,'seq'=4,'blk'=2,'rep'=2] {'blk'}, use_global_device_ids=true, to_apply=%region_18.19 | all-reduce | flops 12 | bytes 96 | tf_op jit(solution)/shard_map/psum | solution.py:168
  94.1 1.4 fusion.4
  95.5 8.3 %all-reduce.2 = bf16[4,2560]{1,0:T(4,128)(2,1)S(1)} all-reduce(bf16[4,2560]{1,0:T(4,128)(2,1)S(1)} %fusion.4), channel_id=3, replica_groups=mesh['grp'=2,'seq'=4,'blk'=2,'rep'=2] {'blk'}, use_global_device_ids=true, to_apply=%region_19.20.clone | all-reduce | flops 10240 | bytes 40960
  105.9 1.6 fusion.44
  108.7 2.1 %convolution_bitcast_fusion.3 = f32[512,1,128]{0,2,1:T(8,128)} fusion(bf16[1,2048,1,128]{3,1,2,0:T(8,128)(2,1)} %copy-done.19, bf16[1,512,512]{1,2,0:T(8,128)(2,1)S(1)} %fusion.55, f32[512]{0:T(512)S(1)} %fusion.39, f32[512]{0:T(512)S(1)} %bitcast.284, f32[512]{0:T(512)S(1)} %get-tuple-element.152), kind=kOutput, calls=%fused_computation.62 | convolution fusion | flops 68681728 | bytes 923648 | tf_op jit(solution)/shard_map/htu,thd->uhd/dot_general | solution.py:245
  111.4 0.8 fusion.22
  112.6 1.3 fusion.88
  113.9 0.9 copy-done.8
  115.5 0.9 fusion.56
  117.9 1.1 pad_maximum_fusion
  119.0 2.5 %copy.61 = f32[2048,128]{1,0:T(8,128)} copy(f32[2048,128]{0,1:T(8,128)} %pad_maximum_fusion) | data formatting | bytes 2097152 | tf_op jit(solution)/shard_map/concatenate | solution.py:252
  121.5 1.3 copy.62
  122.9 1.6 fusion.42
  124.5 2.9 %fusion.49 = bf16[4,512,128]{2,1,0:T(8,128)(2,1)} fusion(f32[4,512,128]{2,1,0:T(8,128)} %bitcast.251, bf16[512,4,128]{2,0,1:T(8,128)(2,1)} %copy-done.15, f32[4,512]{1,0:T(4,128)S(1)} %div.160, f32[4,512]{1,0:T(4,128)} %get-tuple-element.151, f32[128]{0:T(128)} %param.32, f32[4,512]{1,0:T(4,128)} %get-tuple-element.149), kind=kLoop, calls=%fused_computation.87 | loop fusion | flops 1835008 | bytes 2122240 | tf_op jit(solution)/shard_map/convert_element_type | solution.py:62
  127.4 2.1 %copy.54 = bf16[4,512,128]{1,2,0:T(8,128)(2,1)} copy(bf16[4,512,128]{2,1,0:T(8,128)(2,1)} %fusion.49) | data formatting | bytes 1048576 | tf_op jit(solution)/shard_map/convert_element_type | solution.py:62
  129.5 4.2 %all-to-all-start.3 = ((bf16[4,512,128]{1,2,0:T(8,128)(2,1)}), bf16[4,512,128]{1,2,0:T(8,128)(2,1)}, u32[]{:S(2)}, u32[]{:S(2)}) async-start(bf16[4,512,128]{1,2,0:T(8,128)(2,1)} %copy.54), calls=%async_computation.3 | async-start | bytes 1048576 | tf_op jit(solution)/shard_map/all_to_all | solution.py:264
  133.7 1.3 copy.63
  135.1 2.0 %fusion.33 = f32[2048,1,128]{0,2,1:T(8,128)S(1)} fusion(f32[2048,1,128]{0,2,1:T(8,128)S(1)} %scatter-add.25, bf16[1,2048,1,128]{3,1,2,0:T(8,128)(2,1)} %copy-done.19, bf16[1,512,1024]{2,1,0:T(8,128)(2,1)} %copy-done.12, f32[512]{0:T(512)} %copy-done.42, f32[1024]{0:T(1024)} %bitcast.281, f32[512]{0:T(512)} %get-tuple-element.155), kind=kOutput, calls=%fused_computation.61 | convolution fusion | flops 137494528 | bytes 2236416 | tf_op jit(solution)/shard_map/htu,thd->uhd/dot_general | solution.py:245
  137.2 0.9 fusion.12
  140.3 3.8 %collective-permute-start.2 = (bf16[512,128]{1,0:T(8,128)(2,1)S(1)}, bf16[512,128]{1,0:T(8,128)(2,1)S(1)}, u32[]{:S(2)}, u32[]{:S(2)}) collective-permute-start(bf16[512,128]{1,0:T(8,128)(2,1)S(1)} %get-tuple-element.146), channel_id=1, source_target_pairs={{0,12},{4,8},{8,4},{12,0},{1,13},{5,9},{9,5},{13,1},{2,14},{6,10},... | collective-permute-start | bytes 393224 | tf_op jit(solution)/shard_map/ppermute | solution.py:39
  144.8 5.0 %all-gather.2 = bf16[4,1,128]{2,1,0:T(2,128)(2,1)S(1)} all-gather(bf16[1,1,128]{2,1,0:T(2,128)(2,1)S(1)} %bitcast.287), channel_id=2, replica_groups=mesh['grp'=2,'seq'=4,'blk'=2,'rep'=2] {'blk','rep'}, dimensions={0}, use_global_device_ids=true | all-gather | bytes 1280 | tf_op jit(solution)/shard_map/all_gather | solution.py:209
  149.9 5.2 %all-gather.3 = bf16[4,1,2560]{2,1,0:T(2,128)(2,1)S(1)} all-gather(bf16[1,1,2560]{2,1,0:T(2,128)(2,1)S(1)} %bitcast.276), channel_id=1, replica_groups=mesh['grp'=2,'seq'=4,'blk'=2,'rep'=2] {'blk','rep'}, dimensions={0}, use_global_device_ids=true | all-gather | bytes 25600 | tf_op jit(solution)/shard_map/all_gather | solution.py:210
  155.1 1.1 multiply_convert_fusion
  156.2 5.0 %all-to-all-start.4 = ((bf16[4,512,128]{2,1,0:T(8,128)(2,1)}), bf16[4,512,128]{2,1,0:T(8,128)(2,1)S(1)}, u32[]{:S(2)}, u32[]{:S(2)}) async-start(bf16[4,512,128]{2,1,0:T(8,128)(2,1)} %multiply_convert_fusion), calls=%async_computation.4 | async-start | bytes 1048576 | tf_op jit(solution)/shard_map/all_to_all | solution.py:266
  161.7 1.2 convolution_convert_fusion
  163.6 0.8 gather_fusion
  165.1 2.0 %copy.60 = bf16[1,512,512]{2,1,0:T(8,128)(2,1)} copy(bf16[1,512,512]{1,2,0:T(8,128)(2,1)} %bitcast.63) | data formatting | bytes 1048576
  167.2 9.0 %all-to-all-done.4 = bf16[4,512,128]{2,1,0:T(8,128)(2,1)S(1)} async-done(((bf16[4,512,128]{2,1,0:T(8,128)(2,1)}), bf16[4,512,128]{2,1,0:T(8,128)(2,1)S(1)}, u32[]{:S(2)}, u32[]{:S(2)}) %all-to-all-start.4) | async-done | bytes 524320 | tf_op jit(solution)/shard_map/all_to_all | solution.py:266
  (190 shorter events, 23.9 us)
Async XLA Ops:
  0.6 62.5 %copy-start = (bf16[128,2560]{1,0:T(8,128)(2,1)S(1)}, bf16[128,2560]{1,0:T(8,128)(2,1)}, u32[]{:S(2)}) copy-start(bf16[128,2560]{1,0:T(8,128)(2,1)} %param.34) | copy-start | bytes 1966084
  0.6 26.4 %copy-start.57 = (u32[32]{0:T(128)S(1)}, u32[32]{0:T(128)}, u32[]{:S(2)}) copy-start(u32[32]{0:T(128)} %constant.285) | copy-start | bytes 388
  0.7 8.3 %copy-start.22 = (bf16[1,512,512]{2,1,0:T(8,128)(2,1)S(1)}, bf16[1,512,512]{2,1,0:T(8,128)(2,1)}, u32[]{:S(2)}) copy-start(bf16[1,512,512]{2,1,0:T(8,128)(2,1)} %param.29) | copy-start | bytes 1572868
  0.7 28.9 %copy-start.21 = (bf16[128,2560]{1,0:T(8,128)(2,1)S(1)}, bf16[128,2560]{1,0:T(8,128)(2,1)}, u32[]{:S(2)}) copy-start(bf16[128,2560]{1,0:T(8,128)(2,1)} %param.36) | copy-start | bytes 1966084
  2.7 20.8 %all-to-all-start.1 = ((bf16[512,4,128]{0,2,1:T(8,128)(2,1)}), bf16[512,4,128]{0,2,1:T(8,128)(2,1)S(1)}, u32[]{:S(2)}, u32[]{:S(2)}) async-start(bf16[512,4,128]{0,2,1:T(8,128)(2,1)} %broadcast_in_dim.25), calls=%async_computation.1 | async-start | bytes 1048576 | tf_op jit(solution)/shard_map/all_to_all | solution.py:88
  23.5 17.4 %all-to-all-start = ((bf16[512,4,128]{0,2,1:T(8,128)(2,1)}), bf16[512,4,128]{0,2,1:T(8,128)(2,1)S(1)}, u32[]{:S(2)}, u32[]{:S(2)}) async-start(bf16[512,4,128]{0,2,1:T(8,128)(2,1)} %bitcast), calls=%async_computation | async-start | bytes 1048576 | tf_op jit(solution)/shard_map/all_to_all | solution.py:87
  26.9 14.0 %copy-start.26 = (bf16[1,512,128]{2,1,0:T(8,128)(2,1)S(1)}, bf16[1,512,128]{2,1,0:T(8,128)(2,1)}, u32[]{:S(2)}) copy-start(bf16[1,512,128]{2,1,0:T(8,128)(2,1)} %param.31) | copy-start | bytes 393220
  30.8 17.1 %copy-start.3 = (f32[512,4,128]{2,0,1:T(8,128)}, f32[512,4,128]{2,0,1:T(8,128)S(1)}, u32[]{:S(2)}) copy-start(f32[512,4,128]{2,0,1:T(8,128)S(1)} %convert_element_type.405) | copy-start | bytes 3145732
  41.8 5.7 %copy-start.32 = (f32[128]{0:T(128)S(1)}, f32[128]{0:T(128)}, u32[]{:S(2)}) copy-start(f32[128]{0:T(128)} %param.32) | copy-start | bytes 1540
  41.8 18.3 %all-to-all-start.2 = ((bf16[512,4,128]{2,0,1:T(8,128)(2,1)}), bf16[512,4,128]{2,0,1:T(8,128)(2,1)}, u32[]{:S(2)}, u32[]{:S(2)}) async-start(bf16[512,4,128]{2,0,1:T(8,128)(2,1)} %broadcast_in_dim.29), calls=%async_computation.2 | async-start | bytes 1048576 | tf_op jit(solution)/shard_map/all_to_all | solution.py:89
  46.3 3.0 %copy-start.15 = (bf16[512,4,128]{2,0,1:T(8,128)(2,1)}, bf16[512,4,128]{2,0,1:T(8,128)(2,1)S(1)}, u32[]{:S(2)}) copy-start(bf16[512,4,128]{2,0,1:T(8,128)(2,1)S(1)} %copy.49) | copy-start | bytes 1572868
  47.9 4.5 %copy-start.19 = (bf16[1,2048,1,128]{3,1,2,0:T(8,128)(2,1)}, bf16[1,2048,1,128]{3,1,2,0:T(8,128)(2,1)S(1)}, u32[]{:S(2)}) copy-start(bf16[1,2048,1,128]{3,1,2,0:T(8,128)(2,1)S(1)} %multiply_convert_fusion.2) | copy-start | bytes 1572868
  52.4 2.4 %copy-start.12 = (bf16[1,512,1024]{2,1,0:T(8,128)(2,1)}, bf16[1,512,1024]{2,1,0:T(8,128)(2,1)S(1)}, u32[]{:S(2)}) copy-start(bf16[1,512,1024]{2,1,0:T(8,128)(2,1)S(1)} %fusion.50) | copy-start | bytes 3145732
  53.9 1.9 %copy-start.7 = (bf16[1,512,1536]{2,1,0:T(8,128)(2,1)}, bf16[1,512,1536]{2,1,0:T(8,128)(2,1)S(1)}, u32[]{:S(2)}) copy-start(bf16[1,512,1536]{2,1,0:T(8,128)(2,1)S(1)} %fusion.27) | copy-start | bytes 4718596
  57.7 28.9 %copy-start.56 = (f32[128,4]{0,1:T(4,128)S(1)}, f32[128,4]{0,1:T(4,128)}, u32[]{:S(2)}) copy-start(f32[128,4]{0,1:T(4,128)} %param.37) | copy-start | bytes 6148
  88.6 19.3 %copy-start.52 = (f32[128]{0:T(128)}, f32[128]{0:T(128)S(1)}, u32[]{:S(2)}) copy-start(f32[128]{0:T(128)S(1)} %get-tuple-element.139) | copy-start | bytes 1540
  88.6 19.3 %copy-start.54 = (f32[128]{0:T(128)}, f32[128]{0:T(128)S(1)}, u32[]{:S(2)}) copy-start(f32[128]{0:T(128)S(1)} %get-tuple-element.141) | copy-start | bytes 1540
  94.1 9.7 %copy-start.46 = (f32[4]{0:T(128)}, f32[4]{0:T(128)S(1)}, u32[]{:S(2)}) copy-start(f32[4]{0:T(128)S(1)} %get-tuple-element.142) | copy-start | bytes 52
  94.1 9.7 %copy-start.48 = (f32[4]{0:T(128)}, f32[4]{0:T(128)S(1)}, u32[]{:S(2)}) copy-start(f32[4]{0:T(128)S(1)} %get-tuple-element.143) | copy-start | bytes 52
  105.1 3.1 %copy-start.27 = (bf16[1,2560]{1,0:T(2,128)(2,1)}, bf16[1,2560]{1,0:T(2,128)(2,1)S(1)}, u32[]{:S(2)}) copy-start(bf16[1,2560]{1,0:T(2,128)(2,1)S(1)} %subtract_multiply_fusion) | copy-start | bytes 15364
  105.1 3.1 %copy-start.24 = (bf16[1,2048,1,128]{3,1,2,0:T(8,128)(2,1)S(1)}, bf16[1,2048,1,128]{3,1,2,0:T(8,128)(2,1)}, u32[]{:S(2)}) copy-start(bf16[1,2048,1,128]{3,1,2,0:T(8,128)(2,1)} %copy-done.23) | copy-start | bytes 1572868
  108.0 8.4 %copy-start.31 = (f32[1,1024]{1,0:T(1,128)}, f32[1,1024]{1,0:T(1,128)S(1)}, u32[]{:S(2)}) copy-start(f32[1,1024]{1,0:T(1,128)S(1)} %slice.263) | copy-start | bytes 12292
  108.6 8.5 %copy-start.16 = (f32[128,512]{1,0:T(8,128)}, f32[128,512]{1,0:T(8,128)S(1)}, u32[]{:S(2)}) copy-start(f32[128,512]{1,0:T(8,128)S(1)} %fusion.60) | copy-start | bytes 786436
  112.6 2.6 %copy-start.1 = (bf16[512,2048]{1,0:T(8,128)(2,1)}, bf16[512,2048]{1,0:T(8,128)(2,1)S(1)}, u32[]{:S(2)}) copy-start(bf16[512,2048]{1,0:T(8,128)(2,1)S(1)} %fusion.22) | copy-start | bytes 6291460
  112.6 2.2 %copy-start.8 = (bf16[1,512,1536]{2,1,0:T(8,128)(2,1)S(1)}, bf16[1,512,1536]{2,1,0:T(8,128)(2,1)}, u32[]{:S(2)}) copy-start(bf16[1,512,1536]{2,1,0:T(8,128)(2,1)} %copy-done.7) | copy-start | bytes 4718596
  112.6 2.6 %copy-start.13 = (bf16[1,512,1024]{2,1,0:T(8,128)(2,1)S(1)}, bf16[1,512,1024]{2,1,0:T(8,128)(2,1)}, u32[]{:S(2)}) copy-start(bf16[1,512,1024]{2,1,0:T(8,128)(2,1)} %copy-done.12) | copy-start | bytes 3145732
  117.9 3.7 %copy-start.10 = (f32[512,4,128]{2,0,1:T(8,128)S(1)}, f32[512,4,128]{2,0,1:T(8,128)}, u32[]{:S(2)}) copy-start(f32[512,4,128]{2,0,1:T(8,128)} %copy-done.9) | copy-start | bytes 3145732
  124.5 9.2 %copy-start.6 = (f32[512,4,128]{2,0,1:T(8,128)S(1)}, f32[512,4,128]{2,0,1:T(8,128)}, u32[]{:S(2)}) copy-start(f32[512,4,128]{2,0,1:T(8,128)} %copy-done.3) | copy-start | bytes 3145732
  127.4 7.6 %copy-start.25 = (f32[512,1,128]{0,2,1:T(8,128)S(1)}, f32[512,1,128]{0,2,1:T(8,128)}, u32[]{:S(2)}) copy-start(f32[512,1,128]{0,2,1:T(8,128)} %convolution_bitcast_fusion.3) | copy-start | bytes 786436
  129.5 26.7 %all-to-all-start.3 = ((bf16[4,512,128]{1,2,0:T(8,128)(2,1)}), bf16[4,512,128]{1,2,0:T(8,128)(2,1)}, u32[]{:S(2)}, u32[]{:S(2)}) async-start(bf16[4,512,128]{1,2,0:T(8,128)(2,1)} %copy.54), calls=%async_computation.3 | async-start | bytes 1048576 | tf_op jit(solution)/shard_map/all_to_all | solution.py:264
  135.0 2.1 %copy-start.20 = (bf16[1,2048,1,128]{3,1,2,0:T(8,128)(2,1)S(1)}, bf16[1,2048,1,128]{3,1,2,0:T(8,128)(2,1)}, u32[]{:S(2)}) copy-start(bf16[1,2048,1,128]{3,1,2,0:T(8,128)(2,1)} %copy-done.19) | copy-start | bytes 1572868
  135.0 2.1 %copy-start.41 = (f32[512]{0:T(512)S(1)}, f32[512]{0:T(512)}, u32[]{:S(2)}) copy-start(f32[512]{0:T(512)} %copy-done.40) | copy-start | bytes 6148
  135.0 2.1 %copy-start.44 = (f32[512]{0:T(512)S(1)}, f32[512]{0:T(512)}, u32[]{:S(2)}) copy-start(f32[512]{0:T(512)} %get-tuple-element.154) | copy-start | bytes 6148
  137.2 1.8 %copy-start.14 = (f32[2048,1,128]{0,2,1:T(8,128)S(1)}, f32[2048,1,128]{0,2,1:T(8,128)}, u32[]{:S(2)}) copy-start(f32[2048,1,128]{0,2,1:T(8,128)} %copy.63) | copy-start | bytes 3145732
  139.7 5.1 %copy-start.29 = (f32[2048]{0:T(1024)S(1)}, f32[2048]{0:T(1024)}, u32[]{:S(2)}) copy-start(f32[2048]{0:T(1024)} %get-tuple-element.171) | copy-start | bytes 24580
  139.7 5.1 %copy-start.39 = (bf16[128]{0:T(256)(128)(2,1)S(1)}, bf16[128]{0:T(256)(128)(2,1)}, u32[]{:S(2)}) copy-start(bf16[128]{0:T(256)(128)(2,1)} %copy-done.38) | copy-start | bytes 772
  139.7 10.1 %copy-start.28 = (bf16[1,2560]{1,0:T(2,128)(2,1)S(1)}, bf16[1,2560]{1,0:T(2,128)(2,1)}, u32[]{:S(2)}) copy-start(bf16[1,2560]{1,0:T(2,128)(2,1)} %copy-done.27) | copy-start | bytes 15364
  139.7 15.3 %copy-start.37 = (f32[128]{0:T(128)S(1)}, f32[128]{0:T(128)}, u32[]{:S(2)}) copy-start(f32[128]{0:T(128)} %copy-done.36) | copy-start | bytes 1540
  139.9 21.3 %copy-start.51 = (f32[128]{0:T(128)S(1)}, f32[128]{0:T(128)}, u32[]{:S(2)}) copy-start(f32[128]{0:T(128)} %get-tuple-element.137) | copy-start | bytes 1540
  139.9 21.3 %copy-start.53 = (f32[128]{0:T(128)S(1)}, f32[128]{0:T(128)}, u32[]{:S(2)}) copy-start(f32[128]{0:T(128)} %copy-done.52) | copy-start | bytes 1540
  139.9 21.3 %copy-start.55 = (f32[128]{0:T(128)S(1)}, f32[128]{0:T(128)}, u32[]{:S(2)}) copy-start(f32[128]{0:T(128)} %copy-done.54) | copy-start | bytes 1540
  140.0 23.0 %copy-start.47 = (f32[4]{0:T(128)S(1)}, f32[4]{0:T(128)}, u32[]{:S(2)}) copy-start(f32[4]{0:T(128)} %copy-done.46) | copy-start | bytes 52
  140.0 23.0 %copy-start.49 = (f32[4]{0:T(128)S(1)}, f32[4]{0:T(128)}, u32[]{:S(2)}) copy-start(f32[4]{0:T(128)} %copy-done.48) | copy-start | bytes 52
  140.0 23.0 %copy-start.50 = (f32[4]{0:T(128)S(1)}, f32[4]{0:T(128)}, u32[]{:S(2)}) copy-start(f32[4]{0:T(128)} %get-tuple-element.144) | copy-start | bytes 52
  140.3 23.2 %collective-permute-start.2 = (bf16[512,128]{1,0:T(8,128)(2,1)S(1)}, bf16[512,128]{1,0:T(8,128)(2,1)S(1)}, u32[]{:S(2)}, u32[]{:S(2)}) collective-permute-start(bf16[512,128]{1,0:T(8,128)(2,1)S(1)} %get-tuple-element.146), channel_id=1, source_target_pairs={{0,12},{4,8},{8,4},{12,0},{1,13},{5,9},{9,5},{13,1},{2,14},{6,10},... | collective-permute-start | bytes 393224 | tf_op jit(solution)/shard_map/ppermute | solution.py:39
  144.2 19.4 %collective-permute-start.1 = (bf16[512,128]{1,0:T(8,128)(2,1)S(1)}, bf16[512,128]{1,0:T(8,128)(2,1)S(1)}, u32[]{:S(2)}, u32[]{:S(2)}) collective-permute-start(bf16[512,128]{1,0:T(8,128)(2,1)S(1)} %get-tuple-element.147), channel_id=1, source_target_pairs={{0,8},{4,12},{8,0},{12,4},{1,9},{5,13},{9,1},{13,5},{2,10},{6,14},... | collective-permute-start | bytes 393224 | tf_op jit(solution)/shard_map/ppermute | solution.py:39
  144.2 19.4 %collective-permute-start = (bf16[512,128]{1,0:T(8,128)(2,1)S(1)}, bf16[512,128]{1,0:T(8,128)(2,1)S(1)}, u32[]{:S(2)}, u32[]{:S(2)}) collective-permute-start(bf16[512,128]{1,0:T(8,128)(2,1)S(1)} %get-tuple-element.148), channel_id=1, source_target_pairs={{0,4},{4,0},{8,12},{12,8},{1,5},{5,1},{9,13},{13,9},{2,6},{6,2},{1... | collective-permute-start | bytes 393224 | tf_op jit(solution)/shard_map/ppermute | solution.py:39
  156.2 20.0 %all-to-all-start.4 = ((bf16[4,512,128]{2,1,0:T(8,128)(2,1)}), bf16[4,512,128]{2,1,0:T(8,128)(2,1)S(1)}, u32[]{:S(2)}, u32[]{:S(2)}) async-start(bf16[4,512,128]{2,1,0:T(8,128)(2,1)} %multiply_convert_fusion), calls=%async_computation.4 | async-start | bytes 1048576 | tf_op jit(solution)/shard_map/all_to_all | solution.py:266
  (18 other events, 19.5 us)
